TPU v7x, 32 devices: a whole 2x2x4 slice. The times are simulated.
32 devices in a mesh: ctx: 16 (over z, y, x), head: 2 (over core).
Axes of the slice: x: 2, y: 2, z: 4, core: 2. Of those that a mesh axis runs over, the one named last changes fastest.
Arguments:
- queries: bfloat16 [4096, 1024], P('ctx', 'head'), may hold values from -4 to 4
- key_rows: bfloat16 [4096, 1024], P('ctx', 'head'), may hold values from -4 to 4
- value_rows: bfloat16 [4096, 1024], P('ctx', 'head'), may hold values from -6 to 6
- out_grad: bfloat16 [4096, 1024], P('ctx', 'head'), may hold values from -6 to 6
- offsets: int32 [3, 4], P(None, 'head'), may hold values from 0 to 63
Outputs:
- query_grad: bfloat16 [4096, 1024], P('ctx', 'head')
- key_grad: bfloat16 [4096, 1024], P('ctx', 'head')
- value_grad: bfloat16 [4096, 1024], P('ctx', 'head')
All inputs are finite; a program needn't handle non-finite values.
Results may differ from a plain program's by a relative error of at most 0.0068.
Values may be sent and summed in bfloat16 or wider, within the bound.
A program may use at most 128 MiB of HBM per device.

v0:
```python
import jax
import jax.numpy as jnp
from jax import lax
from jax.sharding import PartitionSpec as P

HD = 256
LEVELS = 3
R0 = 1
R1 = 16
R2 = 64
W0 = 2048
W1 = 32768


NEGATIVE = -1e30


def swapped(array, axis, apart):
    return lax.ppermute(array, axis, [(i, i ^ 1 << apart) for i in range(lax.axis_size(axis))])


def pick_rows(field, offset_row, rate):
    folded = field.reshape((field.shape[0] // rate, rate) + field.shape[1:])
    chosen = jnp.arange(rate, dtype=jnp.int32)[:, None] == (offset_row % rate)[None, :]
    chosen = chosen.reshape((1, rate, offset_row.shape[0]) + (1,) * (field.ndim - 2))
    return jnp.sum(jnp.where(chosen, folded, jnp.zeros((), field.dtype)), axis=1)


def place_rows(selected, offset_row, rate, fill):
    chosen = jnp.arange(rate, dtype=jnp.int32)[:, None] == (offset_row % rate)[None, :]
    chosen = chosen.reshape((1, rate, offset_row.shape[0]) + (1,) * (selected.ndim - 2))
    spread = jnp.where(chosen, selected[:, None], jnp.asarray(fill, selected.dtype))
    return spread.reshape((selected.shape[0] * rate,) + selected.shape[1:])


def doubling(stacked, bits, place_no, trade):
    for bit_no in range(bits):
        other = trade(stacked, bit_no)
        on_top = place_no // (1 << bit_no) % 2 == 1
        stacked = jnp.where(
            on_top,
            jnp.concatenate((other, stacked), axis=1),
            jnp.concatenate((stacked, other), axis=1),
        )
    return stacked


def trade_pairs(parcel, bit_no):
    return swapped(parcel, "ctx", bit_no)


def trade_queries(parcel, bit_no):
    return swapped(parcel, "ctx", bit_no)


def trade_stats(parcel, bit_no):
    return swapped(parcel, "ctx", bit_no)


def on_device(queries, key_rows, value_rows, out_grad, offsets):
    tokens_dev, columns = queries.shape
    heads_here = columns // HD
    axis_len = lax.axis_size("ctx")
    device = lax.axis_index("ctx")
    scale = HD ** (-0.5)
    query_all = queries.reshape(tokens_dev, heads_here, HD)
    key_all = key_rows.reshape(tokens_dev, heads_here, HD)
    value_all = value_rows.reshape(tokens_dev, heads_here, HD)
    grad_all = out_grad.reshape(tokens_dev, heads_here, HD)
    rates = (R0, R1, R2)
    spans = (min(W0 // tokens_dev, axis_len), min(W1 // tokens_dev, axis_len), axis_len)
    saved = []
    maxima, sums, partials = ([], [], [])
    for level_no in range(LEVELS):
        rate, span = (rates[level_no], spans[level_no])
        bits = span.bit_length() - 1
        offset_row = offsets[level_no]
        place_no = device % span
        query_pick = pick_rows(query_all, offset_row, rate)
        own_pair = jnp.stack(
            (pick_rows(key_all, offset_row, rate), pick_rows(value_all, offset_row, rate))
        )
        if span == axis_len:
            pair_group = lax.all_gather(own_pair, "ctx", axis=1, tiled=True)
        else:
            pair_group = doubling(own_pair, bits, place_no, trade_pairs)
        scores = (
            jnp.einsum(
                "qhd,khd->hqk", query_pick, pair_group[0], preferred_element_type=jnp.float32
            )
            * scale
        )
        row_max = jnp.max(scores, axis=2)
        weights = jnp.exp(scores - row_max[:, :, None])
        row_sum = jnp.sum(weights, axis=2)
        partial_value = jnp.einsum(
            "hqk,khd->qhd",
            weights.astype(jnp.bfloat16),
            pair_group[1],
            preferred_element_type=jnp.float32,
        )
        maxima.append(place_rows(row_max.T, offset_row, rate, NEGATIVE))
        sums.append(place_rows(row_sum.T, offset_row, rate, 0.0))
        partials.append(place_rows(partial_value, offset_row, rate, 0.0))
        saved.append((query_pick, own_pair, pair_group, scores))
    top = maxima[0]
    for level_no in range(1, LEVELS):
        top = jnp.maximum(top, maxima[level_no])
    total = jnp.zeros_like(top)
    for level_no in range(LEVELS):
        total = total + jnp.exp(maxima[level_no] - top) * sums[level_no]
    lse = top + jnp.log(total)
    combined = jnp.zeros((tokens_dev, heads_here, HD), jnp.float32)
    for level_no in range(LEVELS):
        combined = combined + jnp.exp(maxima[level_no] - lse)[:, :, None] * partials[level_no]
    delta = jnp.sum(grad_all.astype(jnp.float32) * combined, axis=2)
    dquery_all = jnp.zeros((tokens_dev, heads_here, HD), jnp.float32)
    dkey_all = jnp.zeros((tokens_dev, heads_here, HD), jnp.float32)
    dvalue_all = jnp.zeros((tokens_dev, heads_here, HD), jnp.float32)
    for level_no in range(LEVELS):
        rate, span = (rates[level_no], spans[level_no])
        bits = span.bit_length() - 1
        offset_row = offsets[level_no]
        place_no = device % span
        query_pick, own_pair, pair_group, scores = saved[level_no]
        grad_pick = pick_rows(grad_all, offset_row, rate)
        lse_pick = pick_rows(lse, offset_row, rate)
        delta_pick = pick_rows(delta, offset_row, rate)
        probs = jnp.exp(scores - lse_pick.T[:, :, None])
        dprob = jnp.einsum(
            "qhd,khd->hqk", grad_pick, pair_group[1], preferred_element_type=jnp.float32
        )
        dscore = (probs * (dprob - delta_pick.T[:, :, None])).astype(jnp.bfloat16)
        dquery_pick = scale * jnp.einsum(
            "hqk,khd->qhd", dscore, pair_group[0], preferred_element_type=jnp.float32
        )
        query_group = doubling(jnp.stack((query_pick, grad_pick)), bits, place_no, trade_queries)
        stats_group = doubling(jnp.stack((lse_pick, delta_pick)), bits, place_no, trade_stats)
        key_scores = (
            jnp.einsum(
                "qhd,khd->hqk", query_group[0], own_pair[0], preferred_element_type=jnp.float32
            )
            * scale
        )
        key_probs = jnp.exp(key_scores - stats_group[0].T[:, :, None])
        key_dprob = jnp.einsum(
            "qhd,khd->hqk", query_group[1], own_pair[1], preferred_element_type=jnp.float32
        )
        key_dscore = (key_probs * (key_dprob - stats_group[1].T[:, :, None])).astype(jnp.bfloat16)
        dkey_own = scale * jnp.einsum(
            "hqk,qhd->khd", key_dscore, query_group[0], preferred_element_type=jnp.float32
        )
        dvalue_own = jnp.einsum(
            "hqk,qhd->khd",
            key_probs.astype(jnp.bfloat16),
            query_group[1],
            preferred_element_type=jnp.float32,
        )
        own_grads = jnp.stack((dkey_own, dvalue_own))
        dquery_all = dquery_all + place_rows(dquery_pick, offset_row, rate, 0.0)
        dkey_all = dkey_all + place_rows(own_grads[0], offset_row, rate, 0.0)
        dvalue_all = dvalue_all + place_rows(own_grads[1], offset_row, rate, 0.0)
    return (
        dquery_all.reshape(tokens_dev, columns).astype(jnp.bfloat16),
        dkey_all.reshape(tokens_dev, columns).astype(jnp.bfloat16),
        dvalue_all.reshape(tokens_dev, columns).astype(jnp.bfloat16),
    )


def solution(mesh):
    in_specs = (
        P("ctx", "head"),
        P("ctx", "head"),
        P("ctx", "head"),
        P("ctx", "head"),
        P(None, "head"),
    )
    out_specs = (P("ctx", "head"), P("ctx", "head"), P("ctx", "head"))
    return jax.shard_map(
        on_device, mesh=mesh, in_specs=in_specs, out_specs=out_specs, check_vma=False
    )
```

profile of v0, /device:TPU:0, one launch (start us, length us, event | category | flops | bytes accessed | tf_op | source)
XLA Modules:
  0.0 263.4 jit_solution(1361224206526548614)
XLA Ops:
  3.3 3.0 %collective-permute-start = (bf16[2,256,2,256]{3,1,2,0:T(8,128)(2,1)S(1)}, bf16[2,256,2,256]{3,1,2,0:T(8,128)(2,1)}, u32[]{:S(2)}, u32[]{:S(2)}) collective-permute-start(bf16[2,256,2,256]{3,1,2,0:T(8,128)(2,1)S(1)} %pad_maximum_fusion), channel_id=1, source_target_pairs={{0,2},{2,0},{4,6},{6,4},{8,10},{10,8},{12,14},{14,12},{16,18},{18,... | collective-permute-start | bytes 1572872 | tf_op jit(solution)/shard_map/ppermute | solution.py:19
  12.2 2.0 collective-permute-start.3
  16.1 3.0 %collective-permute-done = bf16[2,256,2,256]{3,1,2,0:T(8,128)(2,1)} collective-permute-done((bf16[2,256,2,256]{3,1,2,0:T(8,128)(2,1)S(1)}, bf16[2,256,2,256]{3,1,2,0:T(8,128)(2,1)}, u32[]{:S(2)}, u32[]{:S(2)}) %collective-permute-start) | collective-permute-done | bytes 524320 | tf_op jit(solution)/shard_map/ppermute | solution.py:19
  19.1 1.4 maximum_select_fusion.4
  20.6 2.2 collective-permute-start.1
  22.7 42.1 %all_gather.7 = bf16[2,64,2,256]{3,2,0,1:T(2,128)(2,1)S(1)} all-gather(bf16[2,4,2,256]{3,2,0,1:T(2,128)(2,1)S(1)} %copy.82), channel_id=1, replica_groups=mesh['ctx'=16,'head'=2] {'ctx'}, dimensions={1}, use_global_device_ids=true | all-gather | bytes 139264 | tf_op jit(solution)/shard_map/all_gather | solution.py:84
  65.1 42.0 %all_gather.6 = bf16[2,256,2,256]{3,1,2,0:T(8,128)(2,1)} all-gather(bf16[2,16,2,256]{3,1,2,0:T(8,128)(2,1)S(1)} %pad_maximum_fusion.2), channel_id=1, replica_groups=mesh['ctx'=16,'head'=2] {'ctx'}, dimensions={1}, use_global_device_ids=true | all-gather | bytes 557056 | tf_op jit(solution)/shard_map/all_gather | solution.py:84
  107.2 2.1 maximum_select_fusion.2
  111.3 1.8 convolution_bitcast_fusion.1
  113.1 1.8 maximum_select_fusion.5
  115.8 2.1 collective-permute-start.10
  117.9 1.4 maximum_select_fusion.15
  119.4 11.1 %collective-permute-done.10 = bf16[2,32,2,256]{3,1,2,0:T(8,128)(2,1)S(1)} collective-permute-done((bf16[2,32,2,256]{3,1,2,0:T(8,128)(2,1)S(1)}, bf16[2,32,2,256]{3,1,2,0:T(8,128)(2,1)S(1)}, u32[]{:S(2)}, u32[]{:S(2)}) %collective-permute-start.10) | collective-permute-done | bytes 65568 | tf_op jit(solution)/shard_map/ppermute | solution.py:19
  130.5 2.1 collective-permute-start.11
  137.6 11.9 %collective-permute-done.11 = bf16[2,64,2,256]{3,1,2,0:T(8,128)(2,1)} collective-permute-done((bf16[2,64,2,256]{3,1,2,0:T(8,128)(2,1)S(1)}, bf16[2,64,2,256]{3,1,2,0:T(8,128)(2,1)}, u32[]{:S(2)}, u32[]{:S(2)}) %collective-permute-start.11) | collective-permute-done | bytes 131104 | tf_op jit(solution)/shard_map/ppermute | solution.py:19
  149.5 1.7 maximum_select_fusion.7
  151.9 2.9 %collective-permute-start.20 = (bf16[2,32,2,256]{3,1,2,0:T(8,128)(2,1)}, bf16[2,32,2,256]{3,1,2,0:T(8,128)(2,1)}, u32[]{:S(2)}, u32[]{:S(2)}) collective-permute-start(bf16[2,32,2,256]{3,1,2,0:T(8,128)(2,1)} %maximum_select_fusion.11), channel_id=1, source_target_pairs={{0,16},{2,18},{4,20},{6,22},{8,24},{10,26},{12,28},{14,30},{16,0},... | collective-permute-start | bytes 196616 | tf_op jit(solution)/shard_map/ppermute | solution.py:19
  158.8 1.6 broadcast_in_dim.447
  160.4 2.0 copy.89
  162.4 1.5 broadcast_in_dim.451
  163.9 2.1 copy.91
  168.1 1.3 broadcast_in_dim.450
  171.3 1.8 copy.96
  173.0 1.6 maximum_select_fusion.9
  174.7 2.1 maximum_select_fusion.6
  176.8 3.4 %maximum_select_fusion.3 = bf16[2,1024,2,256]{3,1,2,0:T(8,128)(2,1)} fusion(bf16[2,512,2,256]{3,1,2,0:T(8,128)(2,1)S(1)} %maximum_select_fusion.5, bf16[2,512,2,256]{3,1,2,0:T(8,128)(2,1)} %collective-permute-done.4, pred[]{:T(512)S(6)} %eq.112), kind=kLoop, calls=%fused_computation.21 | loop fusion | flops 9437184 | bytes 4194305 | tf_op jit(solution)/shard_map/jit(_where)/select_n | solution.py:40
  180.8 3.2 %maximum_select_fusion = bf16[2,2048,2,256]{3,1,2,0:T(8,128)(2,1)S(1)} fusion(bf16[2,1024,2,256]{3,1,2,0:T(8,128)(2,1)S(1)} %maximum_select_fusion.2, bf16[2,1024,2,256]{3,1,2,0:T(8,128)(2,1)} %collective-permute-done.2, pred[]{:T(512)S(6)} %eq.111), kind=kLoop, calls=%fused_computation | loop fusion | flops 18874368 | bytes 8388609 | tf_op jit(solution)/shard_map/jit(_where)/select_n | solution.py:40
  186.0 1.3 copy-done
  187.4 1.4 fusion.35
  190.1 5.2 %fusion.31 = f32[2,256,256]{2,1,0:T(8,128)S(1)} fusion(f32[2,2048,256]{2,1,0:T(8,128)} %copy-done, bf16[256,2,256]{0,2,1:T(8,128)(2,1)S(1)} %bitcast.315, f32[2,256]{1,0:T(2,128)S(1)} %bitcast.328, f32[2,256]{1,0:T(2,128)S(1)} %bitcast.331, bf16[2,2048,2,256]{3,1,2,0:T(8,128)(2,1)} %copy-done.2), kind=kOutput, calls=%fused_computation.35 | convolution fusion | flops 1079115776 | bytes 9179136 | tf_op jit(solution)/shard_map/hqk,khd->qhd/dot_general | solution.py:134
  196.8 11.8 %collective-permute-done.5 = bf16[2,1024,2,256]{3,1,2,0:T(8,128)(2,1)} collective-permute-done((bf16[2,1024,2,256]{3,1,2,0:T(8,128)(2,1)}, bf16[2,1024,2,256]{3,1,2,0:T(8,128)(2,1)}, u32[]{:S(2)}, u32[]{:S(2)}) %collective-permute-start.5) | collective-permute-done | bytes 2097184 | tf_op jit(solution)/shard_map/ppermute | solution.py:19
  208.6 4.8 %maximum_select_fusion.1 = bf16[2,2048,2,256]{3,1,2,0:T(8,128)(2,1)S(1)} fusion(bf16[2,1024,2,256]{3,1,2,0:T(8,128)(2,1)} %maximum_select_fusion.3, bf16[2,1024,2,256]{3,1,2,0:T(8,128)(2,1)} %collective-permute-done.5, pred[]{:T(512)S(6)} %eq.111), kind=kLoop, calls=%fused_computation.1 | loop fusion | flops 18874368 | bytes 8388609 | tf_op jit(solution)/shard_map/jit(_where)/select_n | solution.py:40
  213.4 2.0 copy-done.1
  215.4 2.7 %fusion.17 = f32[2,2048,256]{2,1,0:T(8,128)} fusion(bf16[2,2048,2,256]{3,1,2,0:T(8,128)(2,1)S(1)} %maximum_select_fusion.1, bf16[32,2,8,256]{3,2,1,0:T(8,128)(2,1)S(1)} %bitcast.297), kind=kOutput, calls=%fused_computation.29 | convolution fusion | flops 536870912 | bytes 6553600 | tf_op jit(solution)/shard_map/qhd,khd->hqk/dot_general | solution.py:140
  220.3 1.5 collective-permute-done.22
  221.9 1.2 collective-permute-start.23
  223.7 1.7 collective-permute-done.23
  227.7 2.3 collective-permute-done.24
  230.6 1.6 collective-permute-start.16
  232.7 2.3 collective-permute-done.16
  236.8 1.4 collective-permute-start.7
  238.5 2.0 collective-permute-done.7
  240.5 1.3 collective-permute-start.8
  245.0 5.0 %fusion.6 = f32[2,256,256]{2,1,0:T(8,128)} fusion(f32[2,2048,256]{2,1,0:T(8,128)} %fusion.17, f32[2,2048]{1,0:T(2,128)S(1)} %get-tuple-element.24, bf16[2,2048,2,256]{3,1,2,0:T(8,128)(2,1)} %copy-done.1), kind=kOutput, calls=%fused_computation.14 | convolution fusion | flops 540016640 | bytes 6832128 | tf_op jit(solution)/shard_map/hqk,qhd->khd/dot_general | solution.py:153
  249.9 6.5 %fusion.30 = f32[2,256,256]{2,1,0:T(8,128)} fusion(f32[2,2048,256]{2,1,0:T(8,128)} %fusion.17, f32[2,2048]{1,0:T(2,128)} %get-tuple-element.25, f32[2,2048]{1,0:T(2,128)S(1)} %get-tuple-element.24, bf16[2,2048,2,256]{3,1,2,0:T(8,128)(2,1)} %copy-done.1, bf16[32,2,8,256]{3,2,1,0:T(8,128)(2,1)S(1)} %bitcast.298), kind=kOutput, calls=%fused_computation.34 | convolution fusion | flops 1079115776 | bytes 9207808 | tf_op jit(solution)/shard_map/hqk,qhd->khd/dot_general | solution.py:150
  256.4 2.0 copy.114
  258.5 2.0 copy.124
  260.5 2.9 %add_convert_fusion = (bf16[256,512]{1,0:T(8,128)(2,1)}, bf16[256,512]{1,0:T(8,128)(2,1)}, bf16[256,512]{1,0:T(8,128)(2,1)}) fusion(pred[256,512]{1,0:T(8,128)(4,1)S(1)} %copy.100, f32[256,512]{1,0:T(8,128)S(1)} %bitcast.310, f32[256,512]{1,0:T(8,128)} %copy.124, pred[256,512]{1,0:T(8,128)(4,1)} %copy.96, f32[256,512]{1,0:T(8,128)} %bitcast.312, ...), kind=kLoop, calls=%fused_computation.75 | loop fusion | flops 1966080 | bytes 5767168 | tf_op jit(solution)/shard_map/convert_element_type | solution.py:166
  (257 shorter events, 43.8 us)
Async XLA Ops:
  0.6 7.7 %copy-start.51 = (s32[3,2]{0,1:T(2,128)S(1)}, s32[3,2]{0,1:T(2,128)}, u32[]{:S(2)}) copy-start(s32[3,2]{0,1:T(2,128)} %param.9) | copy-start | bytes 76
  0.6 7.9 %copy-start.3 = (bf16[256,512]{1,0:T(8,128)(2,1)S(1)}, bf16[256,512]{1,0:T(8,128)(2,1)}, u32[]{:S(2)}) copy-start(bf16[256,512]{1,0:T(8,128)(2,1)} %param.5) | copy-start | bytes 786436
  0.7 8.0 %copy-start.6 = (bf16[256,512]{1,0:T(8,128)(2,1)S(1)}, bf16[256,512]{1,0:T(8,128)(2,1)}, u32[]{:S(2)}) copy-start(bf16[256,512]{1,0:T(8,128)(2,1)} %param.8) | copy-start | bytes 786436
  3.0 11.2 %copy-start.4 = (bf16[256,512]{1,0:T(8,128)(2,1)S(1)}, bf16[256,512]{1,0:T(8,128)(2,1)}, u32[]{:S(2)}) copy-start(bf16[256,512]{1,0:T(8,128)(2,1)} %param.6) | copy-start | bytes 786436
  3.2 11.1 %copy-start.7 = (bf16[256,512]{1,0:T(8,128)(2,1)S(1)}, bf16[256,512]{1,0:T(8,128)(2,1)}, u32[]{:S(2)}) copy-start(bf16[256,512]{1,0:T(8,128)(2,1)} %param.7) | copy-start | bytes 786436
  3.3 15.9 %collective-permute-start = (bf16[2,256,2,256]{3,1,2,0:T(8,128)(2,1)S(1)}, bf16[2,256,2,256]{3,1,2,0:T(8,128)(2,1)}, u32[]{:S(2)}, u32[]{:S(2)}) collective-permute-start(bf16[2,256,2,256]{3,1,2,0:T(8,128)(2,1)S(1)} %pad_maximum_fusion), channel_id=1, source_target_pairs={{0,2},{2,0},{4,6},{6,4},{8,10},{10,8},{12,14},{14,12},{16,18},{18,... | collective-permute-start | bytes 1572872 | tf_op jit(solution)/shard_map/ppermute | solution.py:19
  9.6 55.1 %copy-start.20 = (bf16[16,2,256]{2,1,0:T(2,128)(2,1)}, bf16[16,2,256]{2,1,0:T(2,128)(2,1)S(1)}, u32[]{:S(2)}) copy-start(bf16[16,2,256]{2,1,0:T(2,128)(2,1)S(1)} %get-tuple-element.9) | copy-start | bytes 49156
  9.6 55.1 %copy-start.22 = (bf16[16,2,256]{2,1,0:T(2,128)(2,1)}, bf16[16,2,256]{2,1,0:T(2,128)(2,1)S(1)}, u32[]{:S(2)}) copy-start(bf16[16,2,256]{2,1,0:T(2,128)(2,1)S(1)} %get-tuple-element.8) | copy-start | bytes 49156
  10.3 104.7 %collective-permute-start.9 = (bf16[2,16,2,256]{3,1,2,0:T(8,128)(2,1)}, bf16[2,16,2,256]{3,1,2,0:T(8,128)(2,1)}, u32[]{:S(2)}, u32[]{:S(2)}) collective-permute-start(bf16[2,16,2,256]{3,1,2,0:T(8,128)(2,1)} %pad_maximum_fusion.3), channel_id=1, source_target_pairs={{0,2},{2,0},{4,6},{6,4},{8,10},{10,8},{12,14},{14,12},{16,18},{18,... | collective-permute-start | bytes 98312 | tf_op jit(solution)/shard_map/ppermute | solution.py:19
  11.1 96.0 %copy-start.9 = (bf16[1,256,2,256]{3,1,2,0:T(8,128)(2,1)}, bf16[1,256,2,256]{3,1,2,0:T(8,128)(2,1)S(1)}, u32[]{:S(2)}) copy-start(bf16[1,256,2,256]{3,1,2,0:T(8,128)(2,1)S(1)} %copy.104) | copy-start | bytes 786436
  11.3 95.9 %copy-start.10 = (bf16[1,256,2,256]{3,1,2,0:T(8,128)(2,1)}, bf16[1,256,2,256]{3,1,2,0:T(8,128)(2,1)S(1)}, u32[]{:S(2)}) copy-start(bf16[1,256,2,256]{3,1,2,0:T(8,128)(2,1)S(1)} %copy.103) | copy-start | bytes 786436
  12.2 101.0 %collective-permute-start.3 = (bf16[2,256,2,256]{3,1,2,0:T(8,128)(2,1)}, bf16[2,256,2,256]{3,1,2,0:T(8,128)(2,1)}, u32[]{:S(2)}, u32[]{:S(2)}) collective-permute-start(bf16[2,256,2,256]{3,1,2,0:T(8,128)(2,1)} %pad_maximum_fusion.1), channel_id=1, source_target_pairs={{0,2},{2,0},{4,6},{6,4},{8,10},{10,8},{12,14},{14,12},{16,18},{18,... | collective-permute-start | bytes 1572872 | tf_op jit(solution)/shard_map/ppermute | solution.py:19
  16.1 101.9 %collective-permute-start.17 = (bf16[2,4,2,256]{3,1,2,0:T(4,128)(2,1)}, bf16[2,4,2,256]{3,1,2,0:T(4,128)(2,1)}, u32[]{:S(2)}, u32[]{:S(2)}) collective-permute-start(bf16[2,4,2,256]{3,1,2,0:T(4,128)(2,1)} %pad_maximum_fusion.5), channel_id=1, source_target_pairs={{0,2},{2,0},{4,6},{6,4},{8,10},{10,8},{12,14},{14,12},{16,18},{18,... | collective-permute-start | bytes 24584 | tf_op jit(solution)/shard_map/ppermute | solution.py:19
  20.6 86.6 %collective-permute-start.1 = (bf16[2,512,2,256]{3,1,2,0:T(8,128)(2,1)S(1)}, bf16[2,512,2,256]{3,1,2,0:T(8,128)(2,1)}, u32[]{:S(2)}, u32[]{:S(2)}) collective-permute-start(bf16[2,512,2,256]{3,1,2,0:T(8,128)(2,1)S(1)} %maximum_select_fusion.4), channel_id=1, source_target_pairs={{0,4},{2,6},{4,0},{6,2},{8,12},{10,14},{12,8},{14,10},{16,20},{18,... | collective-permute-start | bytes 3145736 | tf_op jit(solution)/shard_map/ppermute | solution.py:19
  64.9 42.3 %copy-start.27 = (bf16[1,64,2,256]{3,2,0,1:T(2,128)(2,1)}, bf16[1,64,2,256]{3,2,0,1:T(2,128)(2,1)S(1)}, u32[]{:S(2)}) copy-start(bf16[1,64,2,256]{3,2,0,1:T(2,128)(2,1)S(1)} %get-tuple-element.23) | copy-start | bytes 196612
  64.9 54.4 %copy-start.25 = (bf16[1,64,2,256]{3,2,0,1:T(2,128)(2,1)}, bf16[1,64,2,256]{3,2,0,1:T(2,128)(2,1)S(1)}, u32[]{:S(2)}) copy-start(bf16[1,64,2,256]{3,2,0,1:T(2,128)(2,1)S(1)} %get-tuple-element.22) | copy-start | bytes 196612
  65.1 54.2 %copy-start.41 = (f32[2,4]{1,0:T(2,128)}, f32[2,4]{1,0:T(2,128)S(1)}, u32[]{:S(2)}) copy-start(f32[2,4]{1,0:T(2,128)S(1)} %get-tuple-element.36) | copy-start | bytes 100
  65.1 54.2 %copy-start.49 = (f32[2,4,64]{2,1,0:T(4,128)}, f32[2,4,64]{2,1,0:T(4,128)S(1)}, u32[]{:S(2)}) copy-start(f32[2,4,64]{2,1,0:T(4,128)S(1)} %get-tuple-element.37) | copy-start | bytes 6148
  109.3 71.5 %collective-permute-start.2 = (bf16[2,1024,2,256]{3,1,2,0:T(8,128)(2,1)S(1)}, bf16[2,1024,2,256]{3,1,2,0:T(8,128)(2,1)}, u32[]{:S(2)}, u32[]{:S(2)}) collective-permute-start(bf16[2,1024,2,256]{3,1,2,0:T(8,128)(2,1)S(1)} %maximum_select_fusion.2), channel_id=1, source_target_pairs={{0,8},{2,10},{4,12},{6,14},{8,0},{10,2},{12,4},{14,6},{16,24},{18,... | collective-permute-start | bytes 6291464 | tf_op jit(solution)/shard_map/ppermute | solution.py:19
  111.3 21.3 %copy-start.17 = (f32[2,16,256]{2,1,0:T(8,128)}, f32[2,16,256]{2,1,0:T(8,128)S(1)}, u32[]{:S(2)}) copy-start(f32[2,16,256]{2,1,0:T(8,128)S(1)} %get-tuple-element.39) | copy-start | bytes 98308
  111.3 21.3 %copy-start.31 = (f32[2,16]{1,0:T(2,128)}, f32[2,16]{1,0:T(2,128)S(1)}, u32[]{:S(2)}) copy-start(f32[2,16]{1,0:T(2,128)S(1)} %get-tuple-element.38) | copy-start | bytes 388
  114.9 61.9 %collective-permute-start.4 = (bf16[2,512,2,256]{3,1,2,0:T(8,128)(2,1)S(1)}, bf16[2,512,2,256]{3,1,2,0:T(8,128)(2,1)}, u32[]{:S(2)}, u32[]{:S(2)}) collective-permute-start(bf16[2,512,2,256]{3,1,2,0:T(8,128)(2,1)S(1)} %maximum_select_fusion.5), channel_id=1, source_target_pairs={{0,4},{2,6},{4,0},{6,2},{8,12},{10,14},{12,8},{14,10},{16,20},{18,... | collective-permute-start | bytes 3145736 | tf_op jit(solution)/shard_map/ppermute | solution.py:19
  115.8 14.6 %collective-permute-start.10 = (bf16[2,32,2,256]{3,1,2,0:T(8,128)(2,1)S(1)}, bf16[2,32,2,256]{3,1,2,0:T(8,128)(2,1)S(1)}, u32[]{:S(2)}, u32[]{:S(2)}) collective-permute-start(bf16[2,32,2,256]{3,1,2,0:T(8,128)(2,1)S(1)} %maximum_select_fusion.10), channel_id=1, source_target_pairs={{0,4},{2,6},{4,0},{6,2},{8,12},{10,14},{12,8},{14,10},{16,20},{18,... | collective-permute-start | bytes 196616 | tf_op jit(solution)/shard_map/ppermute | solution.py:19
  119.3 17.4 %collective-permute-start.18 = (bf16[2,8,2,256]{3,1,2,0:T(8,128)(2,1)}, bf16[2,8,2,256]{3,1,2,0:T(8,128)(2,1)}, u32[]{:S(2)}, u32[]{:S(2)}) collective-permute-start(bf16[2,8,2,256]{3,1,2,0:T(8,128)(2,1)} %maximum_select_fusion.15), channel_id=1, source_target_pairs={{0,4},{2,6},{4,0},{6,2},{8,12},{10,14},{12,8},{14,10},{16,20},{18,... | collective-permute-start | bytes 49160 | tf_op jit(solution)/shard_map/ppermute | solution.py:19
  130.5 19.0 %collective-permute-start.11 = (bf16[2,64,2,256]{3,1,2,0:T(8,128)(2,1)S(1)}, bf16[2,64,2,256]{3,1,2,0:T(8,128)(2,1)}, u32[]{:S(2)}, u32[]{:S(2)}) collective-permute-start(bf16[2,64,2,256]{3,1,2,0:T(8,128)(2,1)S(1)} %maximum_select_fusion.8), channel_id=1, source_target_pairs={{0,8},{2,10},{4,12},{6,14},{8,0},{10,2},{12,4},{14,6},{16,24},{18,... | collective-permute-start | bytes 393224 | tf_op jit(solution)/shard_map/ppermute | solution.py:19
  137.5 13.7 %collective-permute-start.19 = (bf16[2,16,2,256]{3,1,2,0:T(8,128)(2,1)S(1)}, bf16[2,16,2,256]{3,1,2,0:T(8,128)(2,1)S(1)}, u32[]{:S(2)}, u32[]{:S(2)}) collective-permute-start(bf16[2,16,2,256]{3,1,2,0:T(8,128)(2,1)S(1)} %maximum_select_fusion.13), channel_id=1, source_target_pairs={{0,8},{2,10},{4,12},{6,14},{8,0},{10,2},{12,4},{14,6},{16,24},{18,... | collective-permute-start | bytes 98312 | tf_op jit(solution)/shard_map/ppermute | solution.py:19
  151.3 23.4 %collective-permute-start.12 = (bf16[2,128,2,256]{3,1,2,0:T(8,128)(2,1)}, bf16[2,128,2,256]{3,1,2,0:T(8,128)(2,1)}, u32[]{:S(2)}, u32[]{:S(2)}) collective-permute-start(bf16[2,128,2,256]{3,1,2,0:T(8,128)(2,1)} %maximum_select_fusion.7), channel_id=1, source_target_pairs={{0,16},{2,18},{4,20},{6,22},{8,24},{10,26},{12,28},{14,30},{16,0},... | collective-permute-start | bytes 786440 | tf_op jit(solution)/shard_map/ppermute | solution.py:19
  151.9 21.1 %collective-permute-start.20 = (bf16[2,32,2,256]{3,1,2,0:T(8,128)(2,1)}, bf16[2,32,2,256]{3,1,2,0:T(8,128)(2,1)}, u32[]{:S(2)}, u32[]{:S(2)}) collective-permute-start(bf16[2,32,2,256]{3,1,2,0:T(8,128)(2,1)} %maximum_select_fusion.11), channel_id=1, source_target_pairs={{0,16},{2,18},{4,20},{6,22},{8,24},{10,26},{12,28},{14,30},{16,0},... | collective-permute-start | bytes 196616 | tf_op jit(solution)/shard_map/ppermute | solution.py:19
  180.1 28.4 %collective-permute-start.5 = (bf16[2,1024,2,256]{3,1,2,0:T(8,128)(2,1)}, bf16[2,1024,2,256]{3,1,2,0:T(8,128)(2,1)}, u32[]{:S(2)}, u32[]{:S(2)}) collective-permute-start(bf16[2,1024,2,256]{3,1,2,0:T(8,128)(2,1)} %maximum_select_fusion.3), channel_id=1, source_target_pairs={{0,8},{2,10},{4,12},{6,14},{8,0},{10,2},{12,4},{14,6},{16,24},{18,... | collective-permute-start | bytes 6291464 | tf_op jit(solution)/shard_map/ppermute | solution.py:19
  185.6 33.7 %copy-start.30 = (f32[256,2]{0,1:T(2,128)}, f32[256,2]{0,1:T(2,128)S(1)}, u32[]{:S(2)}) copy-start(f32[256,2]{0,1:T(2,128)S(1)} %get-tuple-element.18) | copy-start | bytes 6148
  188.8 30.6 %copy-start.29 = (f32[256,2]{0,1:T(2,128)}, f32[256,2]{0,1:T(2,128)S(1)}, u32[]{:S(2)}) copy-start(f32[256,2]{0,1:T(2,128)S(1)} %fusion.35) | copy-start | bytes 6148
  196.4 21.8 %collective-permute-start.21 = (f32[2,4,2]{1,2,0:T(2,128)S(1)}, f32[2,4,2]{1,2,0:T(2,128)S(1)}, u32[]{:S(2)}, u32[]{:S(2)}) collective-permute-start(f32[2,4,2]{1,2,0:T(2,128)S(1)} %pad_maximum_fusion.8), channel_id=1, source_target_pairs={{0,2},{2,0},{4,6},{6,4},{8,10},{10,8},{12,14},{14,12},{16,18},{18,... | collective-permute-start | bytes 200 | tf_op jit(solution)/shard_map/ppermute | solution.py:19
  196.8 18.6 %copy-start.5 = (bf16[256,512]{1,0:T(8,128)(2,1)S(1)}, bf16[256,512]{1,0:T(8,128)(2,1)}, u32[]{:S(2)}) copy-start(bf16[256,512]{1,0:T(8,128)(2,1)} %param.6) | copy-start | bytes 786436
  213.4 16.7 %copy-start.19 = (bf16[2,64,2,256]{3,1,2,0:T(8,128)(2,1)S(1)}, bf16[2,64,2,256]{3,1,2,0:T(8,128)(2,1)}, u32[]{:S(2)}) copy-start(bf16[2,64,2,256]{3,1,2,0:T(8,128)(2,1)} %maximum_select_fusion.9) | copy-start | bytes 393220
  213.4 16.7 %copy-start.36 = (bf16[4,2,256]{2,1,0:T(2,128)(2,1)S(1)}, bf16[4,2,256]{2,1,0:T(2,128)(2,1)}, u32[]{:S(2)}) copy-start(bf16[4,2,256]{2,1,0:T(2,128)(2,1)} %copy-done.35) | copy-start | bytes 12292
  213.4 16.9 %copy-start.34 = (bf16[4,2,256]{2,1,0:T(2,128)(2,1)S(1)}, bf16[4,2,256]{2,1,0:T(2,128)(2,1)}, u32[]{:S(2)}) copy-start(bf16[4,2,256]{2,1,0:T(2,128)(2,1)} %copy-done.33) | copy-start | bytes 12292
  215.4 19.7 %copy-start.12 = (bf16[2,256,2,256]{3,1,2,0:T(8,128)(2,1)S(1)}, bf16[2,256,2,256]{3,1,2,0:T(8,128)(2,1)}, u32[]{:S(2)}) copy-start(bf16[2,256,2,256]{3,1,2,0:T(8,128)(2,1)} %maximum_select_fusion.6) | copy-start | bytes 1572868
  215.4 22.8 %copy-start.21 = (bf16[16,2,256]{2,1,0:T(2,128)(2,1)S(1)}, bf16[16,2,256]{2,1,0:T(2,128)(2,1)}, u32[]{:S(2)}) copy-start(bf16[16,2,256]{2,1,0:T(2,128)(2,1)} %copy-done.20) | copy-start | bytes 49156
  218.1 5.0 %collective-permute-start.13 = (f32[2,16,2]{1,2,0:T(2,128)S(1)}, f32[2,16,2]{1,2,0:T(2,128)S(1)}, u32[]{:S(2)}, u32[]{:S(2)}) collective-permute-start(f32[2,16,2]{1,2,0:T(2,128)S(1)} %pad_maximum_fusion.7), channel_id=1, source_target_pairs={{0,2},{2,0},{4,6},{6,4},{8,10},{10,8},{12,14},{14,12},{16,18},{18,... | collective-permute-start | bytes 776 | tf_op jit(solution)/shard_map/ppermute | solution.py:19
  218.2 3.6 %collective-permute-start.22 = (f32[2,8,2]{1,2,0:T(2,128)S(1)}, f32[2,8,2]{1,2,0:T(2,128)S(1)}, u32[]{:S(2)}, u32[]{:S(2)}) collective-permute-start(f32[2,8,2]{1,2,0:T(2,128)S(1)} %maximum_select_fusion.21), channel_id=1, source_target_pairs={{0,4},{2,6},{4,0},{6,2},{8,12},{10,14},{12,8},{14,10},{16,20},{18,... | collective-permute-start | bytes 392 | tf_op jit(solution)/shard_map/ppermute | solution.py:19
  219.3 16.7 %collective-permute-start.6 = (f32[2,256,2]{1,2,0:T(2,128)S(1)}, f32[2,256,2]{1,2,0:T(2,128)S(1)}, u32[]{:S(2)}, u32[]{:S(2)}) collective-permute-start(f32[2,256,2]{1,2,0:T(2,128)S(1)} %pad_maximum_fusion.6), channel_id=1, source_target_pairs={{0,2},{2,0},{4,6},{6,4},{8,10},{10,8},{12,14},{14,12},{16,18},{18,... | collective-permute-start | bytes 12296 | tf_op jit(solution)/shard_map/ppermute | solution.py:19
  221.9 3.6 %collective-permute-start.23 = (f32[2,16,2]{1,2,0:T(2,128)S(1)}, f32[2,16,2]{1,2,0:T(2,128)S(1)}, u32[]{:S(2)}, u32[]{:S(2)}) collective-permute-start(f32[2,16,2]{1,2,0:T(2,128)S(1)} %maximum_select_fusion.22), channel_id=1, source_target_pairs={{0,8},{2,10},{4,12},{6,14},{8,0},{10,2},{12,4},{14,6},{16,24},{18,... | collective-permute-start | bytes 776 | tf_op jit(solution)/shard_map/ppermute | solution.py:19
  223.2 3.6 %collective-permute-start.14 = (f32[2,32,2]{1,2,0:T(2,128)S(1)}, f32[2,32,2]{1,2,0:T(2,128)S(1)}, u32[]{:S(2)}, u32[]{:S(2)}) collective-permute-start(f32[2,32,2]{1,2,0:T(2,128)S(1)} %maximum_select_fusion.18), channel_id=1, source_target_pairs={{0,4},{2,6},{4,0},{6,2},{8,12},{10,14},{12,8},{14,10},{16,20},{18,... | collective-permute-start | bytes 1544 | tf_op jit(solution)/shard_map/ppermute | solution.py:19
  225.5 4.5 %collective-permute-start.24 = (f32[2,32,2]{1,2,0:T(2,128)S(1)}, f32[2,32,2]{1,2,0:T(2,128)S(1)}, u32[]{:S(2)}, u32[]{:S(2)}) collective-permute-start(f32[2,32,2]{1,2,0:T(2,128)S(1)} %maximum_select_fusion.23), channel_id=1, source_target_pairs={{0,16},{2,18},{4,20},{6,22},{8,24},{10,26},{12,28},{14,30},{16,0},... | collective-permute-start | bytes 1544 | tf_op jit(solution)/shard_map/ppermute | solution.py:19
  226.9 3.7 %collective-permute-start.15 = (f32[2,64,2]{1,2,0:T(2,128)S(1)}, f32[2,64,2]{1,2,0:T(2,128)S(1)}, u32[]{:S(2)}, u32[]{:S(2)}) collective-permute-start(f32[2,64,2]{1,2,0:T(2,128)S(1)} %maximum_select_fusion.19), channel_id=1, source_target_pairs={{0,8},{2,10},{4,12},{6,14},{8,0},{10,2},{12,4},{14,6},{16,24},{18,... | collective-permute-start | bytes 3080 | tf_op jit(solution)/shard_map/ppermute | solution.py:19
  230.6 4.5 %collective-permute-start.16 = (f32[2,128,2]{1,2,0:T(2,128)S(1)}, f32[2,128,2]{1,2,0:T(2,128)S(1)}, u32[]{:S(2)}, u32[]{:S(2)}) collective-permute-start(f32[2,128,2]{1,2,0:T(2,128)S(1)} %maximum_select_fusion.20), channel_id=1, source_target_pairs={{0,16},{2,18},{4,20},{6,22},{8,24},{10,26},{12,28},{14,30},{16,0},... | collective-permute-start | bytes 6152 | tf_op jit(solution)/shard_map/ppermute | solution.py:19
  236.8 3.7 %collective-permute-start.7 = (f32[2,512,2]{1,2,0:T(2,128)S(1)}, f32[2,512,2]{1,2,0:T(2,128)S(1)}, u32[]{:S(2)}, u32[]{:S(2)}) collective-permute-start(f32[2,512,2]{1,2,0:T(2,128)S(1)} %maximum_select_fusion.16), channel_id=1, source_target_pairs={{0,4},{2,6},{4,0},{6,2},{8,12},{10,14},{12,8},{14,10},{16,20},{18,... | collective-permute-start | bytes 24584 | tf_op jit(solution)/shard_map/ppermute | solution.py:19
  240.5 3.8 %collective-permute-start.8 = (f32[2,1024,2]{1,2,0:T(2,128)S(1)}, f32[2,1024,2]{1,2,0:T(2,128)S(1)}, u32[]{:S(2)}, u32[]{:S(2)}) collective-permute-start(f32[2,1024,2]{1,2,0:T(2,128)S(1)} %maximum_select_fusion.14), channel_id=1, source_target_pairs={{0,8},{2,10},{4,12},{6,14},{8,0},{10,2},{12,4},{14,6},{16,24},{18,... | collective-permute-start | bytes 49160 | tf_op jit(solution)/shard_map/ppermute | solution.py:19
  (31 other events, 92.1 us)
where the time goes:
time: 265 us; the launch traced here: 263 us
  blocking collectives  84.1 us (32%)
  waiting for transfers between devices  49.2 us (19%)
  local copies, waits for them, and re-layouts  38.1 us (14%)
  other arithmetic  37 us (14%)
  matrix products  27.9 us (11%)
  starting transfers between devices  25.4 us (10%)
    all_gather x2, blocking collectives, on_device(): pair_group = lax.all_gather(own_pair, 'ctx', axis=1, tiled=True)  84.1 us
    ppermute x25, waiting for transfers between devices, swapped(): lax.ppermute(array, axis, [(i, i ^ 1 << apart) for i in range(lax.axis_si...  49.2 us
    select_n x25, other arithmetic, doubling(): jnp.where(on_top, jnp.concatenate((other, stacked), axis=1), jnp.concaten...  27.2 us
    ppermute x25, starting transfers between devices, swapped(): lax.ppermute(array, axis, [(i, i ^ 1 << apart) for i in range(lax.axis_si...  25.4 us
    broadcast_in_dim x27, local copies, waits for them, and re-layouts, place_rows(): jnp.where(chosen, selected[:, None], jnp.asarray(fill, selected.dtype))  15.9 us
    unnamed x118, local copies, waits for them, and re-layouts  7.85 us
    dot_general x3, matrix products, on_device(): jnp.einsum('hqk,qhd->khd', key_dscore, query_group[0], preferred_element_...  7.03 us
    dot_general x3, matrix products, on_device(): jnp.einsum('hqk,khd->qhd', dscore, pair_group[0], preferred_element_type=...  5.76 us
  transfers between devices with their start and end apart: 25, of which 11 were waited for; matrix products, arithmetic and copies ran while one was open for 29% of the time, Pallas kernels for 0%

commit v1 on v0

v1 whole, which is shorter than its diff:
```python
import functools
import math

import jax
import jax.numpy as jnp
from jax import lax
from jax.experimental import pallas as pl
from jax.experimental.pallas import tpu as pltpu
from jax.sharding import PartitionSpec as P

HD = 256
R1 = 16
R2 = 64
W0 = 2048
PICK = 32
NEGATIVE = -1e30
SCALE = HD ** (-0.5)
LOG2 = SCALE * math.log2(math.e)
F32 = jnp.float32
BF16 = jnp.bfloat16


def dot_nt(a, b):
    return lax.dot_general(a, b, (((1,), (1,)), ((), ())), preferred_element_type=F32)


def dot_tn(a, b):
    return lax.dot_general(a, b, (((0,), (0,)), ((), ())), preferred_element_type=F32)


def dot_nn(a, b):
    return jnp.dot(a, b, preferred_element_type=F32)


def kernel(
    cubes, far_bits,
    q_ref, k_ref, v_ref, g_ref, off_ref,
    dq_ref, dk_ref, dv_ref,
    qb, gb, kb, vb, picks, pick_stage, stat_mine, stat_peer,
    e_buf, d_buf, ds_buf,
    kv_stage, kv_peer, kv_own, pk_stage, pk_peer, pk_own, far_stage, far_peer,
    q_stage, q_peer, q_own, fin,
    send_sem, recv_sem,
):
    rows = q_ref.shape[0]
    span = 4 * rows
    wide = cubes * 2 * PICK
    me = lax.axis_index("ctx")

    def bit(n):
        return lax.rem(lax.div(me, 1 << n), 2)

    def peer(n):
        return {"ctx": me + (1 << n) * (1 - 2 * bit(n))}

    x, y, z = bit(0), bit(1), bit(2)
    cube = lax.div(me, 8)
    used = []

    def send(src, dst, n):
        slot = len(used)
        copy = pltpu.make_async_remote_copy(
            src_ref=src, dst_ref=dst, send_sem=send_sem.at[slot], recv_sem=recv_sem.at[slot],
            device_id=peer(n), device_id_type=pl.DeviceIdType.MESH,
        )
        copy.start()
        used.append(copy)
        return copy

    def block(a, b):
        return pl.ds(pl.multiple_of((a * 2 + b) * rows, rows), rows)

    def cols(a):
        return pl.ds(pl.multiple_of(a * HD, HD), HD)

    barrier = pltpu.get_barrier_semaphore()
    for n in range(3 + far_bits):
        pl.semaphore_signal(barrier, inc=1, device_id=peer(n), device_id_type=pl.DeviceIdType.MESH)

    def offset(level, head):
        return jnp.where(head == 0, off_ref[level, 0], off_ref[level, 1])

    def one_hot(head, shape, row_dim):
        j = lax.broadcasted_iota(jnp.int32, shape, row_dim)
        p = lax.broadcasted_iota(jnp.int32, shape, 1 - row_dim)
        first = (j < 16) & (p == R1 * j + offset(0, head))
        second = (j >= 16) & (p == R2 * (j - 16) + offset(1, head))
        return jnp.where(first | second, 1.0, 0.0).astype(BF16)

    def head_of(ref, head):
        return jnp.where(head == 0, ref[:, :HD], ref[:, HD:])

    k_own, v_own = head_of(k_ref, z), head_of(v_ref, z)
    hot_other = one_hot(1 - z, (PICK, rows), 0)
    pick_stage[0] = dot_nn(hot_other, head_of(k_ref, 1 - z)).astype(BF16)
    pick_stage[1] = dot_nn(hot_other, head_of(v_ref, 1 - z)).astype(BF16)
    hot_mine = one_hot(z, (PICK, rows), 0)
    picks[x, 0, cube, z] = dot_nn(hot_mine, k_own).astype(BF16)
    picks[x, 1, cube, z] = dot_nn(hot_mine, v_own).astype(BF16)

    pl.semaphore_wait(barrier, 3 + far_bits)

    z_picks = send(pick_stage, picks.at[x, :, cube, z], 2)
    z_k = send(k_ref.at[:, cols(1 - z)], kb.at[block(x, z)], 2)
    x_k = send(k_ref.at[:, cols(z)], kb.at[block(x, z)], 0)
    y_q = send(q_ref.at[:, cols(z)], qb.at[block(y, z)], 1)
    z_q = send(q_ref.at[:, cols(1 - z)], qb.at[block(y, z)], 2)
    x_v = send(v_ref.at[:, cols(z)], vb.at[block(x, z)], 0)
    y_g = send(g_ref.at[:, cols(z)], gb.at[block(y, z)], 1)
    z_v = send(v_ref.at[:, cols(1 - z)], vb.at[block(x, z)], 2)
    z_g = send(g_ref.at[:, cols(1 - z)], gb.at[block(y, z)], 2)
    kb[block(x, z), :] = k_own
    vb[block(x, z), :] = v_own
    qb[block(y, z), :] = head_of(q_ref, z)
    gb[block(y, z), :] = head_of(g_ref, z)

    z_picks.wait_recv()
    for n in range(far_bits):
        group = pl.ds(lax.div(cube, 1 << n) * (1 << n), 1 << n)
        far = send(picks.at[x, :, group], picks.at[x, :, group], 3 + n)
        far.wait_recv()
    x_picks = send(picks.at[x], picks.at[x], 0)
    z_k.wait_recv()
    x_k2 = send(kb.at[block(x, 1 - z)], kb.at[block(x, 1 - z)], 0)
    z_q.wait_recv()
    y_q2 = send(qb.at[block(y, 1 - z)], qb.at[block(y, 1 - z)], 1)
    z_v.wait_recv()
    x_v2 = send(vb.at[block(x, 1 - z)], vb.at[block(x, 1 - z)], 0)
    z_g.wait_recv()
    y_g2 = send(gb.at[block(y, 1 - z)], gb.at[block(y, 1 - z)], 1)

    for copy in (x_picks, x_k, y_q, x_v, y_g, x_k2, y_q2, x_v2, y_g2):
        copy.wait_recv()

    def keys(c):
        return kb[c * rows:(c + 1) * rows, :] if c < 4 else picks[c - 4, 0].reshape(wide, HD)

    def values(c):
        return vb[c * rows:(c + 1) * rows, :] if c < 4 else picks[c - 4, 1].reshape(wide, HD)

    def place(c):
        return pl.ds(c * rows, rows) if c < 4 else pl.ds(span + (c - 4) * wide, wide)

    def forward(i, carry):
        here = pl.ds(pl.multiple_of(i * rows, rows), rows)
        q_now, g_now = qb[here, :], gb[here, :]
        j = lax.rem(lax.broadcasted_iota(jnp.int32, (wide, rows), 0), PICK)
        p = lax.broadcasted_iota(jnp.int32, (wide, rows), 1)
        mask = ((j < 16) & (lax.rem(p, R1) == offset(0, z))) | (
            (j >= 16) & (j < 16 + rows // R2) & (lax.rem(p, R2) == offset(1, z))
        )
        top = jnp.full((1, rows), NEGATIVE, F32)
        for c in range(6):
            s = dot_nt(keys(c), q_now) * LOG2
            if c >= 4:
                s = jnp.where(mask, s, NEGATIVE)
            e_buf[place(c), here] = s
            top = jnp.maximum(top, jnp.max(s, axis=0, keepdims=True))
        total = jnp.zeros((1, rows), F32)
        dotted = jnp.zeros((1, rows), F32)
        for c in range(6):
            e = jnp.exp2(e_buf[place(c), here] - top)
            d = dot_nt(values(c), g_now)
            e_buf[place(c), here] = e
            d_buf[place(c), here] = d
            total += jnp.sum(e, axis=0, keepdims=True)
            dotted += jnp.sum(e * d, axis=0, keepdims=True)
        stat_mine[:, here] = jnp.concatenate((top, total, dotted, jnp.zeros((5, rows), F32)), axis=0)
        return carry

    lax.fori_loop(0, 4, forward, 0)
    send(stat_mine, stat_peer, 1).wait_recv()
    top_a, top_b = stat_mine[0:1, :], stat_peer[0:1, :]
    top = jnp.maximum(top_a, top_b)
    keep_a, keep_b = jnp.exp2(top_a - top), jnp.exp2(top_b - top)
    inverse = 1.0 / (keep_a * stat_mine[1:2, :] + keep_b * stat_peer[1:2, :])
    factor = keep_a * inverse
    delta = (keep_a * stat_mine[2:3, :] + keep_b * stat_peer[2:3, :]) * inverse

    def backward(at):
        probs = e_buf[at, :] * factor
        dscore = (probs * (d_buf[at, :] - delta)).astype(BF16)
        ds_buf[at, :] = dscore
        return dot_nn(dscore, qb[...]) * SCALE, dot_nn(probs.astype(BF16), gb[...])

    def pick_at(a):
        return pl.ds(pl.multiple_of(span + a * wide, wide), wide)

    shape = (cubes, 2, PICK, HD)
    dk, dv = backward(pick_at(1 - x))
    pk_stage[0] = dk.astype(BF16).reshape(shape)
    pk_stage[1] = dv.astype(BF16).reshape(shape)
    x_pk = send(pk_stage, pk_peer, 0)
    x_kv = []
    for b in range(2):
        dk, dv = backward(block(1 - x, b))
        kv_stage[b, 0] = dk.astype(BF16)
        kv_stage[b, 1] = dv.astype(BF16)
        x_kv.append(send(kv_stage.at[b], kv_peer.at[b], 0))
    dk, dv = backward(pick_at(x))
    pk_own[0] = dk.reshape(shape)
    pk_own[1] = dv.reshape(shape)
    for b in range(2):
        dk, dv = backward(block(x, b))
        kv_own[b, 0] = dk
        kv_own[b, 1] = dv

    def dquery(a):
        at = pl.ds(pl.multiple_of(a * 2 * rows, 2 * rows), 2 * rows)
        total = dot_tn(ds_buf[pl.ds(0, span), at], kb[...])
        for c in (4, 5):
            total += dot_tn(ds_buf[place(c), at], keys(c))
        return total * SCALE

    q_stage[...] = dquery(1 - y).astype(BF16)
    y_dq = send(q_stage, q_peer, 1)
    q_own[...] = dquery(y)

    x_pk.wait_recv()
    pk_own[...] += pk_peer[...].astype(F32)
    for n in reversed(range(far_bits)):
        size = 1 << n
        mine = pl.ds(lax.div(cube, size) * size, size)
        low = lax.div(cube, 2 * size) * 2 * size
        other = pl.ds(low + (1 - bit(3 + n)) * size, size)
        far_stage[:, other] = pk_own[:, other].astype(BF16)
        far = send(far_stage.at[:, other], far_peer.at[n, :, pl.ds(0, size)], 3 + n)
        far.wait_recv()
        pk_own[:, mine] += far_peer[n, :, 0:size].astype(F32)

    spread = one_hot(z, (rows, PICK), 1)

    def final(kind, b):
        return kv_own[b, kind] + kv_peer[b, kind].astype(F32) + dot_nn(
            spread, pk_own[kind, cube, b].astype(BF16)
        )

    def final_q(b):
        at = pl.ds(pl.multiple_of(b * rows, rows), rows)
        return q_own[at, :] + q_peer[at, :].astype(F32)

    y_dq.wait_recv()
    fin[2] = final_q(1 - z).astype(BF16)
    last = [send(fin.at[2], dq_ref.at[:, cols(z)], 2)]
    x_kv[0].wait_recv()
    x_kv[1].wait_recv()
    for kind, out in ((0, dk_ref), (1, dv_ref)):
        fin[kind] = final(kind, 1 - z).astype(BF16)
        last.append(send(fin.at[kind], out.at[:, cols(z)], 2))
    dq_ref[:, cols(z)] = final_q(z).astype(BF16)
    dk_ref[:, cols(z)] = final(0, z).astype(BF16)
    dv_ref[:, cols(z)] = final(1, z).astype(BF16)
    for copy in last:
        copy.wait_recv()
    for copy in used:
        copy.wait_send()


def on_device(queries, key_rows, value_rows, out_grad, offsets):
    rows, columns = queries.shape
    axis_len = lax.axis_size("ctx")
    cubes = axis_len // 8
    far_bits = cubes.bit_length() - 1
    assert W0 // rows == 8 and columns == 2 * HD
    rates = jnp.array([[R1], [R2]], jnp.int32)
    offs = offsets[1:] % rates
    wide = cubes * 2 * PICK
    all_keys = 4 * rows + 2 * wide
    slots = 28 + 2 * far_bits
    out = jax.ShapeDtypeStruct((rows, columns), BF16)
    vmem = pl.BlockSpec(memory_space=pltpu.VMEM)
    held = pltpu.VMEM((4 * rows, HD), BF16)
    return pl.pallas_call(
        functools.partial(kernel, cubes, far_bits),
        out_shape=(out, out, out),
        in_specs=[vmem] * 4 + [pl.BlockSpec(memory_space=pltpu.SMEM)],
        out_specs=(vmem, vmem, vmem),
        scratch_shapes=[
            held, held, held, held,
            pltpu.VMEM((2, 2, cubes, 2, PICK, HD), BF16),
            pltpu.VMEM((2, PICK, HD), BF16),
            pltpu.VMEM((8, 4 * rows), F32),
            pltpu.VMEM((8, 4 * rows), F32),
            pltpu.VMEM((all_keys, 4 * rows), F32),
            pltpu.VMEM((all_keys, 4 * rows), F32),
            pltpu.VMEM((all_keys, 4 * rows), BF16),
            pltpu.VMEM((2, 2, rows, HD), BF16),
            pltpu.VMEM((2, 2, rows, HD), BF16),
            pltpu.VMEM((2, 2, rows, HD), F32),
            pltpu.VMEM((2, cubes, 2, PICK, HD), BF16),
            pltpu.VMEM((2, cubes, 2, PICK, HD), BF16),
            pltpu.VMEM((2, cubes, 2, PICK, HD), F32),
            pltpu.VMEM((2, cubes, 2, PICK, HD), BF16),
            pltpu.VMEM((far_bits, 2, cubes // 2, 2, PICK, HD), BF16),
            pltpu.VMEM((2 * rows, HD), BF16),
            pltpu.VMEM((2 * rows, HD), BF16),
            pltpu.VMEM((2 * rows, HD), F32),
            pltpu.VMEM((3, rows, HD), BF16),
            pltpu.SemaphoreType.DMA((slots,)),
            pltpu.SemaphoreType.DMA((slots,)),
        ],
        compiler_params=pltpu.CompilerParams(
            collective_id=0, has_side_effects=True, vmem_limit_bytes=60 * 1024 * 1024
        ),
    )(queries, key_rows, value_rows, out_grad, offs)


def solution(mesh):
    in_specs = (
        P("ctx", "head"),
        P("ctx", "head"),
        P("ctx", "head"),
        P("ctx", "head"),
        P(None, "head"),
    )
    out_specs = (P("ctx", "head"), P("ctx", "head"), P("ctx", "head"))
    return jax.shard_map(
        on_device, mesh=mesh, in_specs=in_specs, out_specs=out_specs, check_vma=False
    )
```

time: 265 us -> 63.3 us (0.24)
  blocking collectives: 84.1 us -> 0 us
  Pallas kernels: 0 us -> 56.8 us
  waiting for transfers between devices: 49.2 us -> 0 us
  other arithmetic: 37 us -> 0.75 us
  local copies, waits for them, and re-layouts: 38.1 us -> 4.87 us
  matrix products: 27.9 us -> 0 us
  starting transfers between devices: 25.4 us -> 0 us
    all_gather x2 -> x0, blocking collectives: 84.1 us -> none  [on_device(): pair_group = lax.all_gather(own_pair, 'ctx', axis=1, tiled=True)]
    pallas_call x0 -> x1, Pallas kernels: none -> 56.8 us  [on_device(): pl.pallas_call(functools.partial(kernel, cubes, far_bits), out_shape=(out...]
    ppermute x25 -> x0, waiting for transfers between devices: 49.2 us -> none  [swapped(): lax.ppermute(array, axis, [(i, i ^ 1 << apart) for i in range(lax.axis_si...]
    dot_general x18 -> x0, matrix products: 27.9 us -> none  [the longest x3 7.03 us: on_device(): jnp.einsum('hqk,qhd->khd', key_dscore, query_group[0], preferred_element_...]
    select_n x26 -> x1, other arithmetic: 27.4 us -> 0.75 us  [on_device(): offs = offsets[1:] % rates]
    ppermute x25 -> x0, starting transfers between devices: 25.4 us -> none  [swapped(): lax.ppermute(array, axis, [(i, i ^ 1 << apart) for i in range(lax.axis_si...]
    broadcast_in_dim x31 -> x0, local copies, waits for them, and re-layouts: 20.8 us -> none  [the longest x27 15.9 us: place_rows(): jnp.where(chosen, selected[:, None], jnp.asarray(fill, selected.dtype))]
    reshape x9 -> x0, local copies, waits for them, and re-layouts: 4.75 us -> none  [the longest x7 4.59 us: place_rows(): return spread.reshape((selected.shape[0] * rate,) + selected.shape[1:])]
  transfers between devices with their start and end apart: 25 -> 0, of which waited for: 11 -> 0; matrix products, arithmetic and copies ran while one was open for 29% -> 0% of each run, Pallas kernels for 0% -> 0%
where the time goes in v1:
time: 63.3 us; the launch traced here: 63.1 us
  Pallas kernels  56.8 us (90%)
  local copies, waits for them, and re-layouts  4.87 us (8%)
  other arithmetic  0.75 us (1%)
  between operations  0.65 us (1%)
    pallas_call x1, Pallas kernels, on_device(): pl.pallas_call(functools.partial(kernel, cubes, far_bits), out_shape=(out...  56.8 us
    unnamed x10, local copies, waits for them, and re-layouts  4.12 us

profile of v1, /device:TPU:0, one launch (start us, length us, event | category | flops | bytes accessed | tf_op | source)
XLA Modules:
  0.0 63.1 jit_solution(16381832712337605568)
XLA Ops:
  0.6 0.8 %slice.3 = s32[2,2]{0,1:T(2,128)S(1)} slice(s32[3,2]{0,1:T(2,128)} %param.10), slice={[1:3], [0:2]} | slice | bytes 32 | tf_op jit(solution)/shard_map/slice | solution.py:266
  1.4 0.0 copy-start.2
  1.4 0.1 copy.10
  1.5 0.6 copy-done.2
  2.0 0.8 %and_select_fusion.off_ref = s32[2,2]{1,0:T(2,128)} fusion(s32[2,2]{1,0:T(2,128)S(1)} %copy.10, s32[2]{0:T(128)S(1)} %copy-done.2), kind=kLoop, calls=%fused_computation | loop fusion | flops 24 | bytes 40 | tf_op jit(solution)/shard_map/jit(remainder)/select_n | solution.py:266
  2.8 56.8 %shard_map.85 = (bf16[256,512]{1,0:T(8,128)(2,1)}, bf16[256,512]{1,0:T(8,128)(2,1)}, bf16[256,512]{1,0:T(8,128)(2,1)}) custom-call(bf16[256,512]{1,0:T(8,128)(2,1)} %q_ref.1, bf16[256,512]{1,0:T(8,128)(2,1)} %k_ref.1, bf16[256,512]{1,0:T(8,128)(2,1)} %v_ref.1, bf16[256,512]{1,0:T(8,128)(2,1)} %g_ref.1, s32[2,2]{1,0:T(2,128)} %and_select_fusion.off_ref), custom_call_target="tpu_custom_call" | custom-call | tf_op jit(solution)/shard_map/pallas_call | solution.py:273
  59.6 0.0 copy-start.1
  59.6 1.7 %copy.14 = bf16[256,512]{1,0:T(8,128)(2,1)} copy(bf16[256,512]{1,0:T(8,128)(2,1)} %get-tuple-element.6) | data formatting | bytes 524288
  61.3 0.0 copy-done.1
  61.3 0.0 copy-start
  61.3 0.7 %copy.15 = bf16[256,512]{1,0:T(8,128)(2,1)} copy(bf16[256,512]{1,0:T(8,128)(2,1)S(1)} %copy-done.1) | data formatting | bytes 524288
  62.0 0.3 copy-done
  62.4 0.7 %copy.16 = bf16[256,512]{1,0:T(8,128)(2,1)} copy(bf16[256,512]{1,0:T(8,128)(2,1)S(1)} %copy-done) | data formatting | bytes 524288
Async XLA Ops:
  1.4 0.7 %copy-start.2 = (s32[2]{0:T(128)S(1)}, s32[2]{0:T(128)}, u32[]{:S(2)}) copy-start(s32[2]{0:T(128)} %constant.13) | copy-start | bytes 28
  59.6 1.7 %copy-start.1 = (bf16[256,512]{1,0:T(8,128)(2,1)S(1)}, bf16[256,512]{1,0:T(8,128)(2,1)}, u32[]{:S(2)}) copy-start(bf16[256,512]{1,0:T(8,128)(2,1)} %get-tuple-element.7) | copy-start | bytes 786436
  61.3 1.0 %copy-start = (bf16[256,512]{1,0:T(8,128)(2,1)S(1)}, bf16[256,512]{1,0:T(8,128)(2,1)}, u32[]{:S(2)}) copy-start(bf16[256,512]{1,0:T(8,128)(2,1)} %get-tuple-element.8) | copy-start | bytes 786436

commit v2 on v1

--- a/solution.py
+++ b/solution.py
@@ -13,6 +13,8 @@
 R2 = 64
 W0 = 2048
 PICK = 32
+PARTS = 2
+AHEAD = 3
 NEGATIVE = -1e30
 SCALE = HD ** (-0.5)
 LOG2 = SCALE * math.log2(math.e)
@@ -38,7 +40,7 @@
     dq_ref, dk_ref, dv_ref,
     qb, gb, kb, vb, picks, pick_stage, stat_mine, stat_peer,
     e_buf, d_buf, ds_buf,
-    kv_stage, kv_peer, kv_own, pk_stage, pk_peer, pk_own, far_stage, far_peer,
+    kv_stage, kv_peer, kv_own, pk_stage, pk_peer, pk_near, pk_own, far_stage, far_peer,
     q_stage, q_peer, q_own, fin,
     send_sem, recv_sem,
 ):
@@ -47,13 +49,16 @@
     wide = cubes * 2 * PICK
     me = lax.axis_index("ctx")
 
-    def bit(n):
-        return lax.rem(lax.div(me, 1 << n), 2)
+    core = lax.axis_index("head")
+    weights = (1 + core, 2 - core, 4) + tuple(8 << n for n in range(far_bits))
+
+    def bit_of(n):
+        return lax.rem(lax.div(me, weights[n]), 2)
 
     def peer(n):
-        return {"ctx": me + (1 << n) * (1 - 2 * bit(n))}
-
-    x, y, z = bit(0), bit(1), bit(2)
+        return {"ctx": me + weights[n] * (1 - 2 * bit_of(n))}
+
+    x, y, z = bit_of(0), bit_of(1), bit_of(2)
     cube = lax.div(me, 8)
     used = []
 
@@ -78,7 +83,8 @@
         pl.semaphore_signal(barrier, inc=1, device_id=peer(n), device_id_type=pl.DeviceIdType.MESH)
 
     def offset(level, head):
-        return jnp.where(head == 0, off_ref[level, 0], off_ref[level, 1])
+        rate = (R1, R2)[level]
+        return lax.rem(jnp.where(head == 0, off_ref[level + 1, 0], off_ref[level + 1, 1]), rate)
 
     def one_hot(head, shape, row_dim):
         j = lax.broadcasted_iota(jnp.int32, shape, row_dim)
@@ -100,37 +106,58 @@
 
     pl.semaphore_wait(barrier, 3 + far_bits)
 
+    part = rows // PARTS
+
+    def piece(a, b, i):
+        return pl.ds(pl.multiple_of((a * 2 + b) * rows + i * part, part), part)
+
+    sources = ((k_ref, kb, x, 0), (q_ref, qb, y, 1), (v_ref, vb, x, 0), (g_ref, gb, y, 1))
+    order = [(pair + kind, i) for pair in (0, 2) for i in range(PARTS) for kind in (0, 1)]
+
+    def start_other(kind, i):
+        ref, buf, a, _ = sources[kind]
+        return send(ref.at[pl.ds(i * part, part), cols(1 - z)], buf.at[piece(a, z, i)], 2)
+
+    def group(n, side):
+        size = 1 << n
+        low = lax.div(cube, 2 * size) * 2 * size
+        mine = bit_of(3 + n)
+        return pl.ds(low + (mine if side else 1 - mine) * size, size)
+
     z_picks = send(pick_stage, picks.at[x, :, cube, z], 2)
-    z_k = send(k_ref.at[:, cols(1 - z)], kb.at[block(x, z)], 2)
-    x_k = send(k_ref.at[:, cols(z)], kb.at[block(x, z)], 0)
-    y_q = send(q_ref.at[:, cols(z)], qb.at[block(y, z)], 1)
-    z_q = send(q_ref.at[:, cols(1 - z)], qb.at[block(y, z)], 2)
-    x_v = send(v_ref.at[:, cols(z)], vb.at[block(x, z)], 0)
-    y_g = send(g_ref.at[:, cols(z)], gb.at[block(y, z)], 1)
-    z_v = send(v_ref.at[:, cols(1 - z)], vb.at[block(x, z)], 2)
-    z_g = send(g_ref.at[:, cols(1 - z)], gb.at[block(y, z)], 2)
+    flying = [start_other(*order[n]) for n in range(AHEAD)]
+    arrivals = []
+    for ref, buf, a, n in sources:
+        arrivals.append(send(ref.at[:, cols(z)], buf.at[block(a, z)], n))
     kb[block(x, z), :] = k_own
     vb[block(x, z), :] = v_own
     qb[block(y, z), :] = head_of(q_ref, z)
     gb[block(y, z), :] = head_of(g_ref, z)
 
     z_picks.wait_recv()
+    far = []
     for n in range(far_bits):
-        group = pl.ds(lax.div(cube, 1 << n) * (1 << n), 1 << n)
-        far = send(picks.at[x, :, group], picks.at[x, :, group], 3 + n)
-        far.wait_recv()
-    x_picks = send(picks.at[x], picks.at[x], 0)
-    z_k.wait_recv()
-    x_k2 = send(kb.at[block(x, 1 - z)], kb.at[block(x, 1 - z)], 0)
-    z_q.wait_recv()
-    y_q2 = send(qb.at[block(y, 1 - z)], qb.at[block(y, 1 - z)], 1)
-    z_v.wait_recv()
-    x_v2 = send(vb.at[block(x, 1 - z)], vb.at[block(x, 1 - z)], 0)
-    z_g.wait_recv()
-    y_g2 = send(gb.at[block(y, 1 - z)], gb.at[block(y, 1 - z)], 1)
-
-    for copy in (x_picks, x_k, y_q, x_v, y_g, x_k2, y_q2, x_v2, y_g2):
+        far.append(send(picks.at[x, :, group(n, True)], picks.at[x, :, group(n, True)], 3 + n))
+        if n < far_bits - 1:
+            far[n].wait_recv()
+            arrivals.append(send(picks.at[x, :, group(n, False)], picks.at[x, :, group(n, False)], 0))
+    for n, (kind, i) in enumerate(order):
+        _, buf, a, link = sources[kind]
+        flying[n].wait_recv()
+        if n + AHEAD < len(order):
+            flying.append(start_other(*order[n + AHEAD]))
+        there = buf.at[piece(a, 1 - z, i)]
+        arrivals.append(send(there, there, link))
+        if n == 1:
+            n = far_bits - 1
+            far[n].wait_recv()
+            arrivals.append(send(picks.at[x, :, group(n, False)], picks.at[x, :, group(n, False)], 0))
+
+    for copy in arrivals:
         copy.wait_recv()
+    for b in range(2):
+        picks[1 - x, 0, cube, b] = dot_nn(hot_mine, kb[block(1 - x, b), :]).astype(BF16)
+        picks[1 - x, 1, cube, b] = dot_nn(hot_mine, vb[block(1 - x, b), :]).astype(BF16)
 
     def keys(c):
         return kb[c * rows:(c + 1) * rows, :] if c < 4 else picks[c - 4, 0].reshape(wide, HD)
@@ -188,68 +215,74 @@
 
     shape = (cubes, 2, PICK, HD)
     dk, dv = backward(pick_at(1 - x))
-    pk_stage[0] = dk.astype(BF16).reshape(shape)
-    pk_stage[1] = dv.astype(BF16).reshape(shape)
-    x_pk = send(pk_stage, pk_peer, 0)
-    x_kv = []
-    for b in range(2):
-        dk, dv = backward(block(1 - x, b))
-        kv_stage[b, 0] = dk.astype(BF16)
-        kv_stage[b, 1] = dv.astype(BF16)
-        x_kv.append(send(kv_stage.at[b], kv_peer.at[b], 0))
+    pk_near[0] = dk.reshape(shape)
+    pk_near[1] = dv.reshape(shape)
+    x_pk = []
+    for n in range(far_bits):
+        there = group(n, False)
+        pk_stage[:, there] = pk_near[:, there].astype(BF16)
+        x_pk.append(send(pk_stage.at[:, there], pk_peer.at[:, there], 0))
+    spread = one_hot(z, (rows, PICK), 1)
+    x_kv = {}
+    for name, b in ((1, 1 - z), (0, z)):
+        for kind, grad in enumerate(backward(block(1 - x, b))):
+            near = dot_nn(spread, pk_near[kind, cube, b].astype(BF16))
+            kv_stage[b, kind] = (grad + near).astype(BF16)
+            x_kv[name, kind] = send(kv_stage.at[b, kind], kv_peer.at[b, kind], 0)
     dk, dv = backward(pick_at(x))
     pk_own[0] = dk.reshape(shape)
     pk_own[1] = dv.reshape(shape)
-    for b in range(2):
+    for b in (1 - z, z):
         dk, dv = backward(block(x, b))
         kv_own[b, 0] = dk
         kv_own[b, 1] = dv
 
-    def dquery(a):
-        at = pl.ds(pl.multiple_of(a * 2 * rows, 2 * rows), 2 * rows)
+    def dquery(a, b):
+        at = block(a, b)
         total = dot_tn(ds_buf[pl.ds(0, span), at], kb[...])
         for c in (4, 5):
             total += dot_tn(ds_buf[place(c), at], keys(c))
         return total * SCALE
 
-    q_stage[...] = dquery(1 - y).astype(BF16)
-    y_dq = send(q_stage, q_peer, 1)
-    q_own[...] = dquery(y)
-
-    x_pk.wait_recv()
-    pk_own[...] += pk_peer[...].astype(F32)
+    y_dq = {}
+    for name, b in ((1, 1 - z), (0, z)):
+        q_stage[b] = dquery(1 - y, b).astype(BF16)
+        y_dq[name] = send(q_stage.at[b], q_peer.at[b], 1)
+    for b in (1 - z, z):
+        q_own[b] = dquery(y, b)
+
+    for n in range(far_bits):
+        there = group(n, False)
+        x_pk[n].wait_recv()
+        pk_own[:, there] += pk_peer[:, there].astype(F32)
     for n in reversed(range(far_bits)):
         size = 1 << n
-        mine = pl.ds(lax.div(cube, size) * size, size)
-        low = lax.div(cube, 2 * size) * 2 * size
-        other = pl.ds(low + (1 - bit(3 + n)) * size, size)
+        mine, other = group(n, True), group(n, False)
         far_stage[:, other] = pk_own[:, other].astype(BF16)
         far = send(far_stage.at[:, other], far_peer.at[n, :, pl.ds(0, size)], 3 + n)
         far.wait_recv()
         pk_own[:, mine] += far_peer[n, :, 0:size].astype(F32)
 
-    spread = one_hot(z, (rows, PICK), 1)
-
     def final(kind, b):
         return kv_own[b, kind] + kv_peer[b, kind].astype(F32) + dot_nn(
             spread, pk_own[kind, cube, b].astype(BF16)
         )
 
     def final_q(b):
-        at = pl.ds(pl.multiple_of(b * rows, rows), rows)
-        return q_own[at, :] + q_peer[at, :].astype(F32)
-
-    y_dq.wait_recv()
+        return q_own[b] + q_peer[b].astype(F32)
+
+    y_dq[1].wait_recv()
     fin[2] = final_q(1 - z).astype(BF16)
     last = [send(fin.at[2], dq_ref.at[:, cols(z)], 2)]
-    x_kv[0].wait_recv()
-    x_kv[1].wait_recv()
     for kind, out in ((0, dk_ref), (1, dv_ref)):
+        x_kv[1, kind].wait_recv()
         fin[kind] = final(kind, 1 - z).astype(BF16)
         last.append(send(fin.at[kind], out.at[:, cols(z)], 2))
+    y_dq[0].wait_recv()
     dq_ref[:, cols(z)] = final_q(z).astype(BF16)
-    dk_ref[:, cols(z)] = final(0, z).astype(BF16)
-    dv_ref[:, cols(z)] = final(1, z).astype(BF16)
+    for kind, out in ((0, dk_ref), (1, dv_ref)):
+        x_kv[0, kind].wait_recv()
+        out[:, cols(z)] = final(kind, z).astype(BF16)
     for copy in last:
         copy.wait_recv()
     for copy in used:
@@ -262,11 +295,9 @@
     cubes = axis_len // 8
     far_bits = cubes.bit_length() - 1
     assert W0 // rows == 8 and columns == 2 * HD
-    rates = jnp.array([[R1], [R2]], jnp.int32)
-    offs = offsets[1:] % rates
     wide = cubes * 2 * PICK
     all_keys = 4 * rows + 2 * wide
-    slots = 28 + 2 * far_bits
+    slots = 6 + 8 * PARTS + 8 + 8 + 4 * far_bits
     out = jax.ShapeDtypeStruct((rows, columns), BF16)
     vmem = pl.BlockSpec(memory_space=pltpu.VMEM)
     held = pltpu.VMEM((4 * rows, HD), BF16)
@@ -290,11 +321,12 @@
             pltpu.VMEM((2, cubes, 2, PICK, HD), BF16),
             pltpu.VMEM((2, cubes, 2, PICK, HD), BF16),
             pltpu.VMEM((2, cubes, 2, PICK, HD), F32),
+            pltpu.VMEM((2, cubes, 2, PICK, HD), F32),
             pltpu.VMEM((2, cubes, 2, PICK, HD), BF16),
             pltpu.VMEM((far_bits, 2, cubes // 2, 2, PICK, HD), BF16),
-            pltpu.VMEM((2 * rows, HD), BF16),
-            pltpu.VMEM((2 * rows, HD), BF16),
-            pltpu.VMEM((2 * rows, HD), F32),
+            pltpu.VMEM((2, rows, HD), BF16),
+            pltpu.VMEM((2, rows, HD), BF16),
+            pltpu.VMEM((2, rows, HD), F32),
             pltpu.VMEM((3, rows, HD), BF16),
             pltpu.SemaphoreType.DMA((slots,)),
             pltpu.SemaphoreType.DMA((slots,)),
@@ -302,7 +334,7 @@
         compiler_params=pltpu.CompilerParams(
             collective_id=0, has_side_effects=True, vmem_limit_bytes=60 * 1024 * 1024
         ),
-    )(queries, key_rows, value_rows, out_grad, offs)
+    )(queries, key_rows, value_rows, out_grad, offsets)
 
 
 def solution(mesh):

time: 63.3 us -> 53.9 us (0.85)
  Pallas kernels: 56.8 us -> 48.3 us
  other arithmetic: 0.75 us -> 0 us
    pallas_call x1, Pallas kernels: 56.8 us -> 48.3 us  [on_device(): pl.pallas_call(functools.partial(kernel, cubes, far_bits), out_shape=(out...]
    select_n x1 -> x0, other arithmetic: 0.75 us -> none  [on_device(): offs = offsets[1:] % rates]
    slice x1 -> x0, local copies, waits for them, and re-layouts: 0.75 us -> none  [on_device(): offs = offsets[1:] % rates]
    unnamed x10 -> x8, local copies, waits for them, and re-layouts: 4.12 us -> 4.8 us
where the time goes in v2:
time: 53.9 us; the launch traced here: 53.7 us
  Pallas kernels  48.3 us (90%)
  local copies, waits for them, and re-layouts  4.8 us (9%)
  between operations  0.65 us (1%)
    pallas_call x1, Pallas kernels, on_device(): pl.pallas_call(functools.partial(kernel, cubes, far_bits), out_shape=(out...  48.3 us
    unnamed x8, local copies, waits for them, and re-layouts  4.8 us

profile of v2, /device:TPU:0, one launch (start us, length us, event | category | flops | bytes accessed | tf_op | source)
XLA Modules:
  0.0 53.7 jit_solution(17549126825569137198)
XLA Ops:
  0.6 1.3 %copy.8.off_ref = s32[3,2]{1,0:T(4,128)} copy(s32[3,2]{0,1:T(2,128)} %param.9) | data formatting | bytes 48 | tf_op args[4]
  2.0 48.3 %shard_map.76 = (bf16[256,512]{1,0:T(8,128)(2,1)}, bf16[256,512]{1,0:T(8,128)(2,1)}, bf16[256,512]{1,0:T(8,128)(2,1)}) custom-call(bf16[256,512]{1,0:T(8,128)(2,1)} %q_ref.1, bf16[256,512]{1,0:T(8,128)(2,1)} %k_ref.1, bf16[256,512]{1,0:T(8,128)(2,1)} %v_ref.1, bf16[256,512]{1,0:T(8,128)(2,1)} %g_ref.1, s32[3,2]{1,0:T(4,128)} %copy.8.off_ref), custom_call_target="tpu_custom_call" | custom-call | tf_op jit(solution)/shard_map/pallas_call | solution.py:304
  50.2 0.0 copy-start.1
  50.2 1.7 %copy.12 = bf16[256,512]{1,0:T(8,128)(2,1)} copy(bf16[256,512]{1,0:T(8,128)(2,1)} %get-tuple-element.6) | data formatting | bytes 524288
  52.0 0.0 copy-done.1
  52.0 0.0 copy-start
  52.0 0.7 %copy.13 = bf16[256,512]{1,0:T(8,128)(2,1)} copy(bf16[256,512]{1,0:T(8,128)(2,1)S(1)} %copy-done.1) | data formatting | bytes 524288
  52.7 0.3 copy-done
  53.0 0.7 %copy.14 = bf16[256,512]{1,0:T(8,128)(2,1)} copy(bf16[256,512]{1,0:T(8,128)(2,1)S(1)} %copy-done) | data formatting | bytes 524288
Async XLA Ops:
  50.2 1.7 %copy-start.1 = (bf16[256,512]{1,0:T(8,128)(2,1)S(1)}, bf16[256,512]{1,0:T(8,128)(2,1)}, u32[]{:S(2)}) copy-start(bf16[256,512]{1,0:T(8,128)(2,1)} %get-tuple-element.7) | copy-start | bytes 786436
  52.0 1.0 %copy-start = (bf16[256,512]{1,0:T(8,128)(2,1)S(1)}, bf16[256,512]{1,0:T(8,128)(2,1)}, u32[]{:S(2)}) copy-start(bf16[256,512]{1,0:T(8,128)(2,1)} %get-tuple-element.8) | copy-start | bytes 786436

commit v3 on v2

--- a/solution.py
+++ b/solution.py
@@ -15,6 +15,8 @@
 PICK = 32
 PARTS = 2
 AHEAD = 3
+FAR_AT = 5
+BATCH = 2
 NEGATIVE = -1e30
 SCALE = HD ** (-0.5)
 LOG2 = SCALE * math.log2(math.e)
@@ -84,7 +86,7 @@
 
     def offset(level, head):
         rate = (R1, R2)[level]
-        return lax.rem(jnp.where(head == 0, off_ref[level + 1, 0], off_ref[level + 1, 1]), rate)
+        return lax.rem(jnp.where(head == 0, off_ref[0, level + 1], off_ref[1, level + 1]), rate)
 
     def one_hot(head, shape, row_dim):
         j = lax.broadcasted_iota(jnp.int32, shape, row_dim)
@@ -148,7 +150,7 @@
             flying.append(start_other(*order[n + AHEAD]))
         there = buf.at[piece(a, 1 - z, i)]
         arrivals.append(send(there, there, link))
-        if n == 1:
+        if n == FAR_AT:
             n = far_bits - 1
             far[n].wait_recv()
             arrivals.append(send(picks.at[x, :, group(n, False)], picks.at[x, :, group(n, False)], 0))
@@ -195,8 +197,13 @@
         stat_mine[:, here] = jnp.concatenate((top, total, dotted, jnp.zeros((5, rows), F32)), axis=0)
         return carry
 
-    lax.fori_loop(0, 4, forward, 0)
-    send(stat_mine, stat_peer, 1).wait_recv()
+    swaps = []
+    for i in range(0, 4, BATCH):
+        lax.fori_loop(i, i + BATCH, forward, 0)
+        here = pl.ds(i * rows, BATCH * rows)
+        swaps.append(send(stat_mine.at[:, here], stat_peer.at[:, here], 1))
+    for copy in swaps:
+        copy.wait_recv()
     top_a, top_b = stat_mine[0:1, :], stat_peer[0:1, :]
     top = jnp.maximum(top_a, top_b)
     keep_a, keep_b = jnp.exp2(top_a - top), jnp.exp2(top_b - top)
@@ -232,6 +239,21 @@
     dk, dv = backward(pick_at(x))
     pk_own[0] = dk.reshape(shape)
     pk_own[1] = dv.reshape(shape)
+    for n in range(far_bits):
+        there = group(n, False)
+        x_pk[n].wait_recv()
+        pk_own[:, there] += pk_peer[:, there].astype(F32)
+
+    def far_start(n):
+        other = group(n, False)
+        far_stage[:, other] = pk_own[:, other].astype(BF16)
+        return send(far_stage.at[:, other], far_peer.at[n, :, pl.ds(0, 1 << n)], 3 + n)
+
+    def far_end(n, copy):
+        copy.wait_recv()
+        pk_own[:, group(n, True)] += far_peer[n, :, 0:1 << n].astype(F32)
+
+    far_first = far_start(far_bits - 1)
     for b in (1 - z, z):
         dk, dv = backward(block(x, b))
         kv_own[b, 0] = dk
@@ -251,18 +273,6 @@
     for b in (1 - z, z):
         q_own[b] = dquery(y, b)
 
-    for n in range(far_bits):
-        there = group(n, False)
-        x_pk[n].wait_recv()
-        pk_own[:, there] += pk_peer[:, there].astype(F32)
-    for n in reversed(range(far_bits)):
-        size = 1 << n
-        mine, other = group(n, True), group(n, False)
-        far_stage[:, other] = pk_own[:, other].astype(BF16)
-        far = send(far_stage.at[:, other], far_peer.at[n, :, pl.ds(0, size)], 3 + n)
-        far.wait_recv()
-        pk_own[:, mine] += far_peer[n, :, 0:size].astype(F32)
-
     def final(kind, b):
         return kv_own[b, kind] + kv_peer[b, kind].astype(F32) + dot_nn(
             spread, pk_own[kind, cube, b].astype(BF16)
@@ -274,6 +284,9 @@
     y_dq[1].wait_recv()
     fin[2] = final_q(1 - z).astype(BF16)
     last = [send(fin.at[2], dq_ref.at[:, cols(z)], 2)]
+    far_end(far_bits - 1, far_first)
+    for n in reversed(range(far_bits - 1)):
+        far_end(n, far_start(n))
     for kind, out in ((0, dk_ref), (1, dv_ref)):
         x_kv[1, kind].wait_recv()
         fin[kind] = final(kind, 1 - z).astype(BF16)
@@ -289,6 +302,22 @@
         copy.wait_send()
 
 
+def settle_kernel(a_in, b_in, c_in, a_out, b_out, c_out):
+    a_out[...] = a_in[...]
+    b_out[...] = b_in[...]
+    c_out[...] = c_in[...]
+
+
+def settle(*grads):
+    vmem = pl.BlockSpec(memory_space=pltpu.VMEM)
+    return pl.pallas_call(
+        settle_kernel,
+        out_shape=tuple(jax.ShapeDtypeStruct(g.shape, g.dtype) for g in grads),
+        in_specs=[vmem] * 3,
+        out_specs=(vmem,) * 3,
+    )(*grads)
+
+
 def on_device(queries, key_rows, value_rows, out_grad, offsets):
     rows, columns = queries.shape
     axis_len = lax.axis_size("ctx")
@@ -301,7 +330,7 @@
     out = jax.ShapeDtypeStruct((rows, columns), BF16)
     vmem = pl.BlockSpec(memory_space=pltpu.VMEM)
     held = pltpu.VMEM((4 * rows, HD), BF16)
-    return pl.pallas_call(
+    grads = pl.pallas_call(
         functools.partial(kernel, cubes, far_bits),
         out_shape=(out, out, out),
         in_specs=[vmem] * 4 + [pl.BlockSpec(memory_space=pltpu.SMEM)],
@@ -334,7 +363,8 @@
         compiler_params=pltpu.CompilerParams(
             collective_id=0, has_side_effects=True, vmem_limit_bytes=60 * 1024 * 1024
         ),
-    )(queries, key_rows, value_rows, out_grad, offsets)
+    )(queries, key_rows, value_rows, out_grad, offsets.T)
+    return settle(*grads)
 
 
 def solution(mesh):

time: 53.9 us -> 51.9 us (0.963)
  local copies, waits for them, and re-layouts: 4.8 us -> 0 us
  Pallas kernels: 48.3 us -> 51.1 us
    unnamed x8 -> x0, local copies, waits for them, and re-layouts: 4.8 us -> none
    pallas_call x0 -> x1, Pallas kernels: none -> 2 us  [settle(): pl.pallas_call(settle_kernel, out_shape=tuple((jax.ShapeDtypeStruct(g.sha...]
    pallas_call x1, Pallas kernels: 48.3 us -> 49.1 us  [on_device(): pl.pallas_call(functools.partial(kernel, cubes, far_bits), out_shape=(out...]
where the time goes in v3:
time: 51.9 us; the launch traced here: 51.7 us
  Pallas kernels  51.1 us (98%)
  between operations  0.64 us (1%)
    pallas_call x1, Pallas kernels, on_device(): pl.pallas_call(functools.partial(kernel, cubes, far_bits), out_shape=(out...  49.1 us
    pallas_call x1, Pallas kernels, settle(): pl.pallas_call(settle_kernel, out_shape=tuple((jax.ShapeDtypeStruct(g.sha...  2 us

profile of v3, /device:TPU:0, one launch (start us, length us, event | category | flops | bytes accessed | tf_op | source)
XLA Modules:
  0.0 51.7 jit_solution(3331626017848590370)
XLA Ops:
  0.6 49.1 %shard_map.76 = (bf16[256,512]{1,0:T(8,128)(2,1)}, bf16[256,512]{1,0:T(8,128)(2,1)}, bf16[256,512]{1,0:T(8,128)(2,1)}) custom-call(bf16[256,512]{1,0:T(8,128)(2,1)} %q_ref.1, bf16[256,512]{1,0:T(8,128)(2,1)} %k_ref.1, bf16[256,512]{1,0:T(8,128)(2,1)} %v_ref.1, bf16[256,512]{1,0:T(8,128)(2,1)} %g_ref.1, s32[2,3]{1,0:T(2,128)} %bitcast.1), custom_call_target="tpu_custom_call" | custom-call | tf_op jit(solution)/shard_map/pallas_call | solution.py:333
  49.7 2.0 %shard_map.77 = (bf16[256,512]{1,0:T(8,128)(2,1)}, bf16[256,512]{1,0:T(8,128)(2,1)}, bf16[256,512]{1,0:T(8,128)(2,1)}) custom-call(bf16[256,512]{1,0:T(8,128)(2,1)} %get-tuple-element.6.a_in, bf16[256,512]{1,0:T(8,128)(2,1)} %get-tuple-element.7.b_in, bf16[256,512]{1,0:T(8,128)(2,1)} %get-tuple-element.8.c_in), custom_call_target="tpu_custom_call" | custom-call | tf_op jit(solution)/shard_map/pallas_call | solution.py:313
